TPU v7x, 128 devices: a whole 4x4x4 slice. The times are simulated.
128 devices in a mesh: blk: 32 (over x_lo, z, y), rep: 4 (over x_hi, core).
Axes of the slice: x: 4 (x_hi: 2, x_lo: 2; x = x_hi * 2 + x_lo), y: 4, z: 4, core: 2. Of those that a mesh axis runs over, the one named last changes fastest.
Arguments:
- embeddings: bfloat16 [65536, 1024], P(('blk', 'rep')), as said below
- doc_ids: int32 [65536], P(('blk', 'rep')), may hold values from 0 to 32767, as said below
- plan: int32 [4, 32], replicated, may hold values from 0 to 31, as said below
Outputs:
- soft_score: float32 [65536], P(('blk', 'rep'))
Inputs may be any that keep to these rules, and one draw needn't show every extreme that they name: plan[r, b] = b XOR m_r, with 4 distinct nonzero round values m_r; so block b meets plan[r, b] and that block meets b in round r. `doc_ids`: each id names exactly two rows of the cluster. `embeddings`: no row is zero.
All inputs are finite; a program needn't handle non-finite values.
Results may differ from a plain program's by a relative error of at most 0.0008.
Values may be sent and summed in bfloat16 or wider, within the bound.
A program may use at most 128 MiB of HBM per device.

v0:
```python
import math

import jax
import jax.numpy as jnp
from jax import lax
from jax.experimental import pallas as pl
from jax.experimental.pallas import tpu as pltpu
from jax.sharding import PartitionSpec as P

MESH = pl.DeviceIdType.MESH
NEG = -1e30
SCALE = 256.0 * math.log2(math.e)
UNSCALE = math.log(2.0) / 256.0
ROWS = 512
SPOTS = 16
CHUNK = 32
HALF = 16
D = 1024
PARTS = 4


def lowest_bit(value):
    return jnp.bitwise_and(value, -value)


def odd_bits(value):
    value = jnp.bitwise_xor(value, jnp.right_shift(value, 4))
    value = jnp.bitwise_xor(value, jnp.right_shift(value, 2))
    value = jnp.bitwise_xor(value, jnp.right_shift(value, 1))
    return jnp.bitwise_and(value, 1)


def chooser(first, second):
    common = jnp.bitwise_and(first, second)
    return jnp.where(
        common != 0,
        lowest_bit(common),
        jnp.bitwise_or(lowest_bit(first), lowest_bit(second)),
    )


def kernel(
    plan,
    emb,
    ids,
    out,
    left,
    held,
    outbox,
    right,
    left_ids,
    id_in,
    id_table,
    scores,
    row_max,
    row_sum,
    row_in,
    col_own,
    col_in,
    col_table,
    one_s,
    one_r,
    rep_s,
    rep_r,
    two_s,
    two_r,
    own_s,
    own_r,
    ida_s,
    ida_r,
    idb_s,
    idb_r,
    row_s,
    row_r,
    cola_s,
    cola_r,
    colb_s,
    colb_r,
):
    blk = lax.axis_index("blk")
    rep = lax.axis_index("rep")
    lo, z, y = blk // 16, (blk // 4) % 4, blk % 4
    hi, core = rep // 2, rep % 2
    here = z * 4 + y

    def at_spot(k):
        return (lo * 16 + ((z + k // 4) % 4) * 4 + (y + k % 4) % 4, rep)

    def spot_to(k):
        return ((z + k // 4) % 4) * 4 + (y + k % 4) % 4

    def spot_from(k):
        return ((z + 4 - k // 4) % 4) * 4 + (y + 4 - k % 4) % 4

    intra = ((1 - lo) * 16 + here, rep)
    inter = ((1 - lo) * 16 + here, (1 - hi) * 2 + core)
    sibling = (blk, hi * 2 + 1 - core)
    across = (blk, (1 - hi) * 2 + core)
    diagonal = (blk, (1 - hi) * 2 + 1 - core)

    def remote(src, dst, send, recv, device):
        return pltpu.make_async_remote_copy(
            src_ref=src,
            dst_ref=dst,
            send_sem=send,
            recv_sem=recv,
            device_id=device,
            device_id_type=MESH,
        )

    def loop(first, last, body):
        def step(k, carry):
            body(k)
            return carry

        lax.fori_loop(first, last, step, jnp.int32(0))

    barrier = pltpu.get_barrier_semaphore()
    for device in (intra, inter, sibling, across, diagonal):
        pl.semaphore_signal(barrier, inc=1, device_id=device, device_id_type=MESH)
    loop(
        1,
        SPOTS,
        lambda k: pl.semaphore_signal(barrier, inc=1, device_id=at_spot(k), device_id_type=MESH),
    )

    def normalize(i):
        rows = pl.ds(pl.multiple_of(i * 64, 64), 64)
        wide = emb[rows, :].astype(jnp.float32)
        total = jnp.sum(wide * wide, axis=1, keepdims=True)
        left[0, rows, :] = (wide * lax.rsqrt(total + 1e-06)).astype(jnp.bfloat16)

    loop(0, ROWS // 64, normalize)
    id_in[0, 0:4, :] = ids[...]
    id_in[0, 4:8, :] = ids[...]
    pl.semaphore_wait(barrier, SPOTS - 1 + 5)

    def spread(k):
        rows = pl.ds(pl.multiple_of(spot_to(k) * CHUNK, CHUNK), CHUNK)
        return remote(
            left.at[0, rows], held.at[0, here], one_s.at[k], one_r.at[k], at_spot(k)
        )

    loop(1, SPOTS, lambda k: spread(k).start())
    held[0, here] = left[0, pl.ds(pl.multiple_of(here * CHUNK, CHUNK), CHUNK), :]

    group = (sibling, across, diagonal, intra, inter)

    def id_copy(j):
        return remote(id_in.at[0], id_in.at[j], ida_s.at[j], ida_r.at[j], group[j - 1])

    for j in range(1, 6):
        id_copy(j).start()

    def to_sibling():
        return remote(left.at[0], left.at[1], own_s.at[0], own_r.at[0], sibling)

    def to_across(i):
        rows = pl.ds(i * (ROWS // PARTS), ROWS // PARTS)
        return remote(
            left.at[0, rows], left.at[2, rows], own_s.at[1 + i], own_r.at[1 + i], across
        )

    def forward(i):
        rows = pl.ds(i * (ROWS // PARTS), ROWS // PARTS)
        j = 1 + PARTS + i
        return remote(left.at[2, rows], left.at[3, rows], own_s.at[j], own_r.at[j], sibling)

    to_sibling().start()
    to_across(0).start()

    def hand(k, side):
        rows = pl.ds(side * HALF, HALF)
        spot = spot_from(k)
        return remote(
            held.at[0, spot, rows],
            held.at[1, spot, rows],
            rep_s.at[side, k],
            rep_r.at[side, k],
            (intra, inter)[side],
        )

    hand(0, 0).start()
    hand(0, 1).start()

    def pass_on(k):
        spread(k).wait_recv()
        hand(k, 0).start()
        hand(k, 1).start()

    loop(1, SPOTS, pass_on)
    for i in range(1, PARTS):
        to_across(i).start()

    for j in range(1, 6):
        id_copy(j).wait_recv()
    lane = lax.broadcasted_iota(jnp.int32, (8, 128), 1)
    first_half = lane % CHUNK < HALF
    beside = jnp.where(first_half, id_in[4], id_in[5])
    id_table[here, 0:4, :] = id_in[0, 0:4, :]
    id_table[here, 4:8, :] = beside[0:4, :]

    def id_spread(k):
        return remote(
            id_table.at[here], id_table.at[here], idb_s.at[k], idb_r.at[k], at_spot(k)
        )

    loop(1, SPOTS, lambda k: id_spread(k).start())

    masks = [plan[r, 0] for r in range(4)]
    choosers = [chooser(masks[0], masks[1]), chooser(masks[2], masks[3])]

    def hosted_mask(pair, block):
        second = odd_bits(jnp.bitwise_and(block, choosers[pair]))
        return jnp.where(second == 1, masks[2 * pair + 1], masks[2 * pair])

    def guest_mask(pair, block):
        second = odd_bits(jnp.bitwise_and(block, choosers[pair]))
        return jnp.where(second == 1, masks[2 * pair], masks[2 * pair + 1])

    def place(mask, spot):
        return jnp.right_shift(mask, 4), jnp.bitwise_xor(spot, jnp.bitwise_and(mask, 15))

    def drain(k):
        hand(k, 0).wait_recv()
        hand(k, 1).wait_recv()

    loop(0, SPOTS, drain)

    def deliver(pair, k):
        return remote(
            outbox.at[pair, k],
            right.at[pair, here],
            two_s.at[pair, k],
            two_r.at[pair, k],
            at_spot(k),
        )

    for pair in range(2):

        def send_rows(k, pair=pair):
            spot = spot_to(k)
            side, source = place(hosted_mask(pair, lo * 16 + spot), spot)
            outbox[pair, k] = held[side, source]
            deliver(pair, k).start()

        loop(1, SPOTS, send_rows)
        side, source = place(hosted_mask(pair, blk), here)
        right[pair, here] = held[side, source]

    for j in range(4):
        for g in range(4):
            wide_ids = jnp.broadcast_to(id_in[j, g : g + 1, :], (128, 128))
            left_ids[pl.ds(j * ROWS + g * 128, 128), :] = wide_ids.T

    loop(1, SPOTS, lambda k: id_spread(k).wait_recv())

    def tile(pair, slot, right_ids, state):
        scores[...] = lax.dot_general(
            left[slot],
            right[pair].reshape(ROWS, D),
            (((1,), (1,)), ((), ())),
            preferred_element_type=jnp.float32,
        )

        def step(i, state):
            tops, sums = state
            rows = pl.ds(pl.multiple_of(i * 64, 64), 64)
            base = pl.ds(pl.multiple_of(slot * ROWS + i * 64, 64), 64)
            own_ids = left_ids[base, :]
            values = []
            for g in range(4):
                part = scores[rows, g * 128 : (g + 1) * 128] * SCALE
                values.append(jnp.where(own_ids == right_ids[g : g + 1, :], NEG, part))
            top = jnp.maximum(
                jnp.maximum(values[0], values[1]), jnp.maximum(values[2], values[3])
            )
            row_max[pair, base, :] = top
            row_sum[pair, base, :] = (
                jnp.exp2(values[0] - top)
                + jnp.exp2(values[1] - top)
                + jnp.exp2(values[2] - top)
                + jnp.exp2(values[3] - top)
            )
            new_tops, new_sums = [], []
            for g in range(4):
                stack = values[g].reshape(8, 8, 128)
                new = jnp.maximum(tops[g], jnp.max(stack, axis=0))
                new_tops.append(new)
                new_sums.append(
                    sums[g] * jnp.exp2(tops[g] - new)
                    + jnp.sum(jnp.exp2(stack - new[None]), axis=0)
                )
            return tuple(new_tops), tuple(new_sums)

        return lax.fori_loop(0, ROWS // 64, step, state)

    def start_state():
        return (
            tuple(jnp.full((8, 128), NEG, jnp.float32) for _ in range(4)),
            tuple(jnp.zeros((8, 128), jnp.float32) for _ in range(4)),
        )

    def picked_ids(pair):
        side, source = place(hosted_mask(pair, blk), here)
        both = id_table[source]
        return jnp.where(side == 1, both[4:8, :], both[0:4, :])

    def finish_columns(pair, state):
        tops, sums = state
        for g in range(4):
            top = jnp.max(tops[g], axis=0, keepdims=True)
            total = jnp.sum(sums[g] * jnp.exp2(tops[g] - top), axis=0, keepdims=True)
            row = pair * 4 + g
            col_own[row : row + 1, :] = top + jnp.log2(total)

    for pair in range(2):
        loop(1, SPOTS, lambda k, pair=pair: deliver(pair, k).wait_recv())
        right_ids = picked_ids(pair)
        if pair == 0:
            to_sibling().wait_recv()
        state = start_state()
        state = tile(pair, 0, right_ids, state)
        state = tile(pair, 1, right_ids, state)
        if pair == 0:
            for i in range(PARTS):
                to_across(i).wait_recv()
                forward(i).start()
        state = tile(pair, 2, right_ids, state)
        if pair == 0:
            for i in range(PARTS):
                forward(i).wait_recv()
        state = tile(pair, 3, right_ids, state)
        finish_columns(pair, state)

    def col_copy(j):
        return remote(col_own, col_in.at[j], cola_s.at[j], cola_r.at[j], (intra, inter)[j])

    col_copy(0).start()
    col_copy(1).start()

    for j in (1, 2, 3, 0):
        for g in range(4):
            base = pl.ds(j * ROWS + g * 128, 128)
            first_top, second_top = row_max[0, base, :].T, row_max[1, base, :].T
            first_sum, second_sum = row_sum[0, base, :].T, row_sum[1, base, :].T
            top = jnp.max(jnp.maximum(first_top, second_top), axis=0, keepdims=True)
            total = jnp.sum(
                first_sum * jnp.exp2(first_top - top) + second_sum * jnp.exp2(second_top - top),
                axis=0,
                keepdims=True,
            )
            row_in[j, g : g + 1, :] = top + jnp.log2(total)

    def row_copy(j):
        return remote(
            row_in.at[j], row_in.at[3 + j], row_s.at[j], row_r.at[j], group[j - 1]
        )

    for j in range(1, 4):
        row_in[j, 4:8, :] = row_in[j, 0:4, :]
        row_copy(j).start()

    for j in range(2):
        col_copy(j).wait_recv()
    col_table[here, 0] = col_own[...]
    col_table[here, 1] = jnp.where(first_half, col_in[0], col_in[1])

    def col_spread(k):
        return remote(
            col_table.at[here], col_table.at[here], colb_s.at[k], colb_r.at[k], at_spot(k)
        )

    loop(1, SPOTS, lambda k: col_spread(k).start())
    loop(1, SPOTS, lambda k: col_spread(k).wait_recv())
    for j in range(1, 4):
        row_copy(j).wait_recv()

    terms = [row_in[0, 0:4, :]]
    for j in range(1, 4):
        terms.append(row_in[3 + j, 0:4, :])
    for pair in range(2):
        side, source = place(guest_mask(pair, blk), here)
        terms.append(col_table[source, side][pair * 4 : pair * 4 + 4, :])
    top = terms[0]
    for term in terms[1:]:
        top = jnp.maximum(top, term)
    total = jnp.exp2(terms[0] - top)
    for term in terms[1:]:
        total = total + jnp.exp2(term - top)
    out[...] = (top + jnp.log2(total)) * UNSCALE

    def sent(k):
        spread(k).wait_send()
        id_spread(k).wait_send()
        deliver(0, k).wait_send()
        deliver(1, k).wait_send()
        col_spread(k).wait_send()

    loop(1, SPOTS, sent)

    def handed(k):
        hand(k, 0).wait_send()
        hand(k, 1).wait_send()

    loop(0, SPOTS, handed)
    to_sibling().wait_send()
    for i in range(PARTS):
        to_across(i).wait_send()
        forward(i).wait_send()
    for j in range(1, 6):
        id_copy(j).wait_send()
    for j in range(1, 4):
        row_copy(j).wait_send()
    for j in range(2):
        col_copy(j).wait_send()


def shards(embeddings, doc_ids, plan):
    vmem = pl.BlockSpec(memory_space=pltpu.VMEM)
    sems = pltpu.SemaphoreType.DMA
    result = pl.pallas_call(
        kernel,
        out_shape=jax.ShapeDtypeStruct((4, 128), jnp.float32),
        in_specs=[pl.BlockSpec(memory_space=pltpu.SMEM), vmem, vmem],
        out_specs=vmem,
        scratch_shapes=[
            pltpu.VMEM((4, ROWS, D), jnp.bfloat16),
            pltpu.VMEM((2, SPOTS, CHUNK, D), jnp.bfloat16),
            pltpu.VMEM((2, SPOTS, CHUNK, D), jnp.bfloat16),
            pltpu.VMEM((2, SPOTS, CHUNK, D), jnp.bfloat16),
            pltpu.VMEM((4 * ROWS, 128), jnp.int32),
            pltpu.VMEM((6, 8, 128), jnp.int32),
            pltpu.VMEM((SPOTS, 8, 128), jnp.int32),
            pltpu.VMEM((ROWS, ROWS), jnp.float32),
            pltpu.VMEM((2, 4 * ROWS, 128), jnp.float32),
            pltpu.VMEM((2, 4 * ROWS, 128), jnp.float32),
            pltpu.VMEM((7, 8, 128), jnp.float32),
            pltpu.VMEM((8, 128), jnp.float32),
            pltpu.VMEM((2, 8, 128), jnp.float32),
            pltpu.VMEM((SPOTS, 2, 8, 128), jnp.float32),
            sems((SPOTS,)),
            sems((SPOTS,)),
            sems((2, SPOTS)),
            sems((2, SPOTS)),
            sems((2, SPOTS)),
            sems((2, SPOTS)),
            sems((1 + 2 * PARTS,)),
            sems((1 + 2 * PARTS,)),
            sems((6,)),
            sems((6,)),
            sems((SPOTS,)),
            sems((SPOTS,)),
            sems((4,)),
            sems((4,)),
            sems((2,)),
            sems((2,)),
            sems((SPOTS,)),
            sems((SPOTS,)),
        ],
        compiler_params=pltpu.CompilerParams(
            collective_id=0, has_side_effects=True, vmem_limit_bytes=56 * 2**20
        ),
        cost_estimate=pl.CostEstimate(
            flops=2 * 4 * ROWS * 2 * ROWS * D,
            bytes_accessed=ROWS * D * 2,
            transcendentals=2 * 4 * ROWS * 2 * ROWS,
        ),
        name="tournament",
    )(plan, embeddings, doc_ids.reshape(4, 128))
    return result.reshape(ROWS)


def solution(mesh):
    placed = (P(("blk", "rep"), None), P(("blk", "rep")), P())
    return jax.shard_map(
        shards, mesh=mesh, in_specs=placed, out_specs=P(("blk", "rep")), check_vma=False
    )
```

profile of v0, /device:TPU:0, one launch (start us, length us, event | category | flops | bytes accessed | tf_op | source)
XLA Modules:
  0.0 80.5 jit_solution(2499845776812304683)
XLA Ops:
  0.0 79.2 %tournament.1 = f32[4,128]{1,0:T(4,128)} custom-call(s32[4,32]{1,0:T(4,128)} %plan.1, bf16[512,1024]{1,0:T(8,128)(2,1)} %emb.1, s32[4,128]{1,0:T(4,128)} %bitcast.3), custom_call_target="tpu_custom_call" | custom-call | flops 4294967296 | bytes 1048576 | tf_op jit(solution)/shard_map/tournament/pallas_call | solution.py:422
  79.2 1.3 %copy.5 = f32[512]{0:T(512)} copy(f32[512]{0:T(512)} %bitcast.2) | data formatting | bytes 4096
where the time goes:
time: 80.8 us; the launch traced here: 80.5 us
  Pallas kernels  79.2 us (98%)
  local copies, waits for them, and re-layouts  1.26 us (2%)
    pallas_call x1, Pallas kernels, shards(): pl.pallas_call(kernel, out_shape=jax.ShapeDtypeStruct((4, 128), jnp.float...  79.2 us

commit v1 on v0

v1 whole, which is shorter than its diff:
```python
import math

import jax
import jax.numpy as jnp
from jax import lax
from jax.experimental import pallas as pl
from jax.experimental.pallas import tpu as pltpu
from jax.sharding import PartitionSpec as P

MESH = pl.DeviceIdType.MESH
NEG = -1e30
SCALE = 256.0 * math.log2(math.e)
UNSCALE = math.log(2.0) / 256.0
ROWS = 512
BLOCKS = 32
SPOTS = 16
WAVES = 2
WAVE_ROWS = ROWS // WAVES
CHUNK = WAVE_ROWS // SPOTS
D = 1024
PARTS = 4
PIECE = ROWS // PARTS


def lowest_bit(value):
    return jnp.bitwise_and(value, -value)


def odd_bits(value):
    value = jnp.bitwise_xor(value, jnp.right_shift(value, 4))
    value = jnp.bitwise_xor(value, jnp.right_shift(value, 2))
    value = jnp.bitwise_xor(value, jnp.right_shift(value, 1))
    return jnp.bitwise_and(value, 1)


def chooser(first, second):
    common = jnp.bitwise_and(first, second)
    return jnp.where(
        common != 0,
        lowest_bit(common),
        jnp.bitwise_or(lowest_bit(first), lowest_bit(second)),
    )


def kernel(
    plan_in,
    emb_in,
    ids_in,
    out,
    plan,
    emb,
    left,
    held_first,
    held_second,
    outbox,
    right,
    left_ids,
    id_in,
    id_table,
    scores,
    row_max,
    row_sum,
    row_in,
    col_max,
    col_sum,
    col_own,
    col_in,
    col_table,
    load_s,
    one_s,
    one_r,
    rep_s,
    rep_r,
    two_s,
    two_r,
    own_s,
    own_r,
    ida_s,
    ida_r,
    idb_s,
    idb_r,
    row_s,
    row_r,
    cola_s,
    cola_r,
    colb_s,
    colb_r,
):
    held = (held_first, held_second)
    blk = lax.axis_index("blk")
    rep = lax.axis_index("rep")
    lo, z, y = blk // 16, (blk // 4) % 4, blk % 4
    hi, core = rep // 2, rep % 2
    here = z * 4 + y

    def at_spot(k):
        return (lo * 16 + ((z + k // 4) % 4) * 4 + (y + k % 4) % 4, rep)

    def spot_to(k):
        return ((z + k // 4) % 4) * 4 + (y + k % 4) % 4

    intra = ((1 - lo) * 16 + here, rep)
    inter = ((1 - lo) * 16 + here, (1 - hi) * 2 + core)
    sibling = (blk, hi * 2 + 1 - core)
    across = (blk, (1 - hi) * 2 + core)
    diagonal = (blk, (1 - hi) * 2 + 1 - core)

    def remote(src, dst, send, recv, device):
        return pltpu.make_async_remote_copy(
            src_ref=src,
            dst_ref=dst,
            send_sem=send,
            recv_sem=recv,
            device_id=device,
            device_id_type=MESH,
        )

    def loop(first, last, body):
        def step(k, carry):
            body(k)
            return carry

        lax.fori_loop(first, last, step, jnp.int32(0))

    barrier = pltpu.get_barrier_semaphore()
    for device in (intra, inter, sibling, across, diagonal):
        pl.semaphore_signal(barrier, inc=1, device_id=device, device_id_type=MESH)
    loop(
        1,
        SPOTS,
        lambda k: pl.semaphore_signal(barrier, inc=1, device_id=at_spot(k), device_id_type=MESH),
    )

    loads = [
        pltpu.make_async_copy(emb_in, emb, load_s.at[0]),
        pltpu.make_async_copy(plan_in, plan, load_s.at[1]),
        pltpu.make_async_copy(ids_in, id_in.at[0, 0:4], load_s.at[2]),
        pltpu.make_async_copy(ids_in, id_in.at[0, 4:8], load_s.at[3]),
    ]
    for load in loads:
        load.start()
    for load in loads:
        load.wait()

    def normalize(i):
        rows = pl.ds(pl.multiple_of(i * 64, 64), 64)
        wide = emb[rows, :].astype(jnp.float32)
        total = jnp.sum(wide * wide, axis=1, keepdims=True)
        left[0, rows, :] = (wide * lax.rsqrt(total + 1e-06)).astype(jnp.bfloat16)

    loop(0, ROWS // 64, normalize)
    pl.semaphore_wait(barrier, SPOTS - 1 + 5)

    def chunk(w, spot):
        return pl.ds(pl.multiple_of(w * WAVE_ROWS + spot * CHUNK, CHUNK), CHUNK)

    def spread(w, k):
        return remote(
            left.at[0, chunk(w, spot_to(k))],
            held[w].at[0, here],
            one_s.at[w, k],
            one_r.at[w, k],
            at_spot(k),
        )

    for w in range(WAVES):
        loop(1, SPOTS, lambda k, w=w: spread(w, k).start())
        held[w][0, here] = left[0, chunk(w, here), :]

    group = (sibling, across, diagonal, intra, inter)

    def id_copy(j):
        return remote(id_in.at[0], id_in.at[j], ida_s.at[j], ida_r.at[j], group[j - 1])

    for j in range(1, 6):
        id_copy(j).start()

    def to_sibling():
        return remote(left.at[0], left.at[1], own_s.at[0], own_r.at[0], sibling)

    def to_across(i):
        rows = pl.ds(i * PIECE, PIECE)
        return remote(
            left.at[0, rows], left.at[2, rows], own_s.at[1 + i], own_r.at[1 + i], across
        )

    def forward(i):
        rows = pl.ds(i * PIECE, PIECE)
        j = 1 + PARTS + i
        return remote(left.at[2, rows], left.at[3, rows], own_s.at[j], own_r.at[j], sibling)

    to_sibling().start()
    to_across(0).start()

    def hand(w, dz):
        from_z = (z + 4 - dz) % 4
        spots = pl.ds(from_z * 4, 4)
        side = (from_z + w) % 2
        return remote(
            held[w].at[0, spots],
            held[w].at[1, spots],
            rep_s.at[w, dz],
            rep_r.at[w, dz],
            ((1 - lo) * 16 + here, ((hi + side) % 2) * 2 + core),
        )

    for w in range(WAVES):
        for dz in (0, 1, 3, 2):
            for dy in range(4):
                if dz or dy:
                    spread(w, dz * 4 + dy).wait_recv()
            hand(w, dz).start()

    for j in range(1, 6):
        id_copy(j).wait_recv()
    id_table[here, 0:4, :] = id_in[0, 0:4, :]
    for w in range(WAVES):
        rows = slice(2 * w, 2 * w + 2)
        id_table[here, 4 + 2 * w : 6 + 2 * w, :] = jnp.where(
            (z + w) % 2 == 0, id_in[4, rows, :], id_in[5, rows, :]
        )

    def id_spread(k):
        return remote(
            id_table.at[here], id_table.at[here], idb_s.at[k], idb_r.at[k], at_spot(k)
        )

    loop(1, SPOTS, lambda k: id_spread(k).start())

    masks = [plan[r, 0] for r in range(4)]
    choosers = [chooser(masks[0], masks[1]), chooser(masks[2], masks[3])]

    def hosted_mask(pair, block):
        second = odd_bits(jnp.bitwise_and(block, choosers[pair]))
        return jnp.where(second == 1, masks[2 * pair + 1], masks[2 * pair])

    def guest_mask(pair, block):
        second = odd_bits(jnp.bitwise_and(block, choosers[pair]))
        return jnp.where(second == 1, masks[2 * pair], masks[2 * pair + 1])

    def place(mask, spot):
        return jnp.right_shift(mask, 4), jnp.bitwise_xor(spot, jnp.bitwise_and(mask, 15))

    def deliver(w, pair, k):
        return remote(
            outbox.at[w, pair, k],
            right.at[w, pair, here],
            two_s.at[w, pair, k],
            two_r.at[w, pair, k],
            at_spot(k),
        )

    def deliver_all(w, pair):
        def send_rows(k):
            spot = spot_to(k)
            side, source = place(hosted_mask(pair, lo * 16 + spot), spot)
            outbox[w, pair, k] = held[w][side, source]
            deliver(w, pair, k).start()

        loop(1, SPOTS, send_rows)
        side, source = place(hosted_mask(pair, blk), here)
        right[w, pair, here] = held[w][side, source]

    for w in range(WAVES):
        for dz in range(4):
            hand(w, dz).wait_recv()
        if w == WAVES - 1:
            for i in range(1, PARTS):
                to_across(i).start()
        for pair in range(2):
            deliver_all(w, pair)

    for j in range(4):
        for g in range(4):
            wide_ids = jnp.broadcast_to(id_in[j, g : g + 1, :], (128, 128))
            left_ids[pl.ds(j * ROWS + g * 128, 128), :] = wide_ids.T

    loop(1, SPOTS, lambda k: id_spread(k).wait_recv())

    def part_ids(w, pair):
        side, source = place(hosted_mask(pair, blk), here)
        both = id_table[source]
        return jnp.where(side == 1, both[4 + 2 * w : 6 + 2 * w, :], both[2 * w : 2 * w + 2, :])

    col_max[...] = jnp.full(col_max.shape, NEG, jnp.float32)
    col_sum[...] = jnp.zeros(col_sum.shape, jnp.float32)

    def tile(w, pair, slot, first, count):
        scores[0:count, :] = lax.dot_general(
            left[slot, first : first + count, :],
            right[w, pair].reshape(WAVE_ROWS, D),
            (((1,), (1,)), ((), ())),
            preferred_element_type=jnp.float32,
        )
        right_ids = part_ids(w, pair)
        part = w * 2 + pair

        def step(i, state):
            tops, sums = state
            rows = pl.ds(i * 64, 64)
            base = pl.ds(slot * ROWS + first + i * 64, 64)
            own_ids = left_ids[base, :]
            values = []
            for g in range(2):
                some = scores[rows, g * 128 : (g + 1) * 128] * SCALE
                values.append(jnp.where(own_ids == right_ids[g : g + 1, :], NEG, some))
            top = jnp.maximum(values[0], values[1])
            if part:
                older = row_max[base, :]
                top = jnp.maximum(top, older)
            total = jnp.exp2(values[0] - top) + jnp.exp2(values[1] - top)
            if part:
                total = total + row_sum[base, :] * jnp.exp2(older - top)
            row_max[base, :] = top
            row_sum[base, :] = total
            new_tops, new_sums = [], []
            for g in range(2):
                stack = values[g].reshape(8, 8, 128)
                new = jnp.maximum(tops[g], jnp.max(stack, axis=0))
                new_tops.append(new)
                new_sums.append(
                    sums[g] * jnp.exp2(tops[g] - new)
                    + jnp.sum(jnp.exp2(stack - new[None]), axis=0)
                )
            return tuple(new_tops), tuple(new_sums)

        state = (
            tuple(col_max[part, :, g * 128 : (g + 1) * 128] for g in range(2)),
            tuple(col_sum[part, :, g * 128 : (g + 1) * 128] for g in range(2)),
        )
        for i in range(count // 64):
            state = step(i, state)
        tops, sums = state
        for g in range(2):
            col_max[part, :, g * 128 : (g + 1) * 128] = tops[g]
            col_sum[part, :, g * 128 : (g + 1) * 128] = sums[g]

    def finish_columns(w, pair):
        part = w * 2 + pair
        tops = col_max[part]
        top = jnp.max(tops, axis=0, keepdims=True)
        total = jnp.sum(col_sum[part] * jnp.exp2(tops - top), axis=0, keepdims=True)
        result = top + jnp.log2(total)
        for g in range(2):
            row = pair * 4 + w * 2 + g
            col_own[row : row + 1, :] = result[:, g * 128 : (g + 1) * 128]

    def arrived(w, pair):
        loop(1, SPOTS, lambda k: deliver(w, pair, k).wait_recv())

    to_across(0).wait_recv()
    forward(0).start()
    to_sibling().wait_recv()
    half = ROWS // 2
    for pair in range(2):
        arrived(0, pair)
        tile(0, pair, 0, 0, ROWS)
        tile(0, pair, 1, 0, ROWS)
    to_across(1).wait_recv()
    forward(1).start()
    for pair in range(2):
        tile(0, pair, 2, 0, half)
    forward(0).wait_recv()
    forward(1).wait_recv()
    for pair in range(2):
        tile(0, pair, 3, 0, half)
    arrived(1, 0)
    tile(1, 0, 0, 0, ROWS)
    tile(1, 0, 1, 0, ROWS)
    tile(1, 0, 2, 0, half)
    tile(1, 0, 3, 0, half)
    for i in range(2, PARTS):
        to_across(i).wait_recv()
        forward(i).start()
    for w, pair in ((0, 0), (0, 1), (1, 0)):
        tile(w, pair, 2, half, half)
    for i in range(2, PARTS):
        forward(i).wait_recv()
    for w, pair in ((0, 0), (0, 1), (1, 0)):
        tile(w, pair, 3, half, half)
        finish_columns(w, pair)
    arrived(1, 1)
    for slot in (1, 2, 3, 0):
        tile(1, 1, slot, 0, ROWS)
    finish_columns(1, 1)

    def col_copy(j):
        return remote(col_own, col_in.at[j], cola_s.at[j], cola_r.at[j], (intra, inter)[j])

    col_copy(0).start()
    col_copy(1).start()

    def row_copy(j):
        return remote(
            row_in.at[j], row_in.at[3 + j], row_s.at[j], row_r.at[j], group[j - 1]
        )

    for j in (1, 2, 3, 0):
        for g in range(4):
            base = pl.ds(j * ROWS + g * 128, 128)
            tops = row_max[base, :].T
            top = jnp.max(tops, axis=0, keepdims=True)
            total = jnp.sum(row_sum[base, :].T * jnp.exp2(tops - top), axis=0, keepdims=True)
            row_in[j, g : g + 1, :] = top + jnp.log2(total)
        if j:
            row_in[j, 4:8, :] = row_in[j, 0:4, :]
            row_copy(j).start()

    for j in range(2):
        col_copy(j).wait_recv()
    col_table[here, 0] = col_own[...]
    for pair in range(2):
        source = place(hosted_mask(pair, (1 - lo) * 16 + here), here)[1]
        odd = jnp.bitwise_and(jnp.right_shift(source, 2), 1)
        for w in range(WAVES):
            rows = slice(pair * 4 + w * 2, pair * 4 + w * 2 + 2)
            col_table[here, 1, rows, :] = jnp.where(
                odd == w, col_in[0, rows, :], col_in[1, rows, :]
            )

    def col_spread(k):
        return remote(
            col_table.at[here], col_table.at[here], colb_s.at[k], colb_r.at[k], at_spot(k)
        )

    loop(1, SPOTS, lambda k: col_spread(k).start())
    loop(1, SPOTS, lambda k: col_spread(k).wait_recv())
    for j in range(1, 4):
        row_copy(j).wait_recv()

    terms = [row_in[0, 0:4, :]]
    for j in range(1, 4):
        terms.append(row_in[3 + j, 0:4, :])
    for pair in range(2):
        side, source = place(guest_mask(pair, blk), here)
        terms.append(col_table[source, side][pair * 4 : pair * 4 + 4, :])
    top = terms[0]
    for term in terms[1:]:
        top = jnp.maximum(top, term)
    total = jnp.exp2(terms[0] - top)
    for term in terms[1:]:
        total = total + jnp.exp2(term - top)
    out[...] = (top + jnp.log2(total)) * UNSCALE

    def sent(k):
        id_spread(k).wait_send()
        for w in range(WAVES):
            spread(w, k).wait_send()
            for pair in range(2):
                deliver(w, pair, k).wait_send()
        col_spread(k).wait_send()

    loop(1, SPOTS, sent)
    for w in range(WAVES):
        for dz in range(4):
            hand(w, dz).wait_send()
    to_sibling().wait_send()
    for i in range(PARTS):
        to_across(i).wait_send()
        forward(i).wait_send()
    for j in range(1, 6):
        id_copy(j).wait_send()
    for j in range(1, 4):
        row_copy(j).wait_send()
    for j in range(2):
        col_copy(j).wait_send()


def shards(embeddings, doc_ids, plan):
    sems = pltpu.SemaphoreType.DMA
    result = pl.pallas_call(
        kernel,
        out_shape=jax.ShapeDtypeStruct((4, 128), jnp.float32),
        in_specs=[pl.BlockSpec(memory_space=pl.ANY)] * 3,
        out_specs=pl.BlockSpec(memory_space=pltpu.VMEM),
        scratch_shapes=[
            pltpu.SMEM((4, BLOCKS), jnp.int32),
            pltpu.VMEM((ROWS, D), jnp.bfloat16),
            pltpu.VMEM((4, ROWS, D), jnp.bfloat16),
            pltpu.VMEM((2, SPOTS, CHUNK, D), jnp.bfloat16),
            pltpu.VMEM((2, SPOTS, CHUNK, D), jnp.bfloat16),
            pltpu.VMEM((WAVES, 2, SPOTS, CHUNK, D), jnp.bfloat16),
            pltpu.VMEM((WAVES, 2, SPOTS, CHUNK, D), jnp.bfloat16),
            pltpu.VMEM((4 * ROWS, 128), jnp.int32),
            pltpu.VMEM((6, 8, 128), jnp.int32),
            pltpu.VMEM((SPOTS, 8, 128), jnp.int32),
            pltpu.VMEM((ROWS, WAVE_ROWS), jnp.float32),
            pltpu.VMEM((4 * ROWS, 128), jnp.float32),
            pltpu.VMEM((4 * ROWS, 128), jnp.float32),
            pltpu.VMEM((7, 8, 128), jnp.float32),
            pltpu.VMEM((4, 8, WAVE_ROWS), jnp.float32),
            pltpu.VMEM((4, 8, WAVE_ROWS), jnp.float32),
            pltpu.VMEM((8, 128), jnp.float32),
            pltpu.VMEM((2, 8, 128), jnp.float32),
            pltpu.VMEM((SPOTS, 2, 8, 128), jnp.float32),
            sems((4,)),
            sems((WAVES, SPOTS)),
            sems((WAVES, SPOTS)),
            sems((WAVES, 4)),
            sems((WAVES, 4)),
            sems((WAVES, 2, SPOTS)),
            sems((WAVES, 2, SPOTS)),
            sems((1 + 2 * PARTS,)),
            sems((1 + 2 * PARTS,)),
            sems((6,)),
            sems((6,)),
            sems((SPOTS,)),
            sems((SPOTS,)),
            sems((4,)),
            sems((4,)),
            sems((2,)),
            sems((2,)),
            sems((SPOTS,)),
            sems((SPOTS,)),
        ],
        compiler_params=pltpu.CompilerParams(
            collective_id=0, has_side_effects=True, vmem_limit_bytes=56 * 2**20
        ),
        cost_estimate=pl.CostEstimate(
            flops=2 * 4 * ROWS * 2 * ROWS * D,
            bytes_accessed=ROWS * D * 2,
            transcendentals=2 * 4 * ROWS * 2 * ROWS,
        ),
        name="tournament",
    )(plan, embeddings, doc_ids.reshape(4, 128))
    return result.reshape(ROWS)


def solution(mesh):
    placed = (P(("blk", "rep"), None), P(("blk", "rep")), P())
    return jax.shard_map(
        shards, mesh=mesh, in_specs=placed, out_specs=P(("blk", "rep")), check_vma=False
    )
```

time: 80.8 us -> 64.1 us (0.79)
  Pallas kernels: 79.2 us -> 62.3 us
    pallas_call x1, Pallas kernels: 79.2 us -> 62.3 us  [shards(): pl.pallas_call(kernel, out_shape=jax.ShapeDtypeStruct((4, 128), jnp.float...]
where the time goes in v1:
time: 64.1 us; the launch traced here: 63.6 us
  Pallas kernels  62.3 us (97%)
  local copies, waits for them, and re-layouts  1.26 us (2%)
    pallas_call x1, Pallas kernels, shards(): pl.pallas_call(kernel, out_shape=jax.ShapeDtypeStruct((4, 128), jnp.float...  62.3 us

profile of v1, /device:TPU:0, one launch (start us, length us, event | category | flops | bytes accessed | tf_op | source)
XLA Modules:
  0.0 63.6 jit_solution(6389084544282760292)
XLA Ops:
  0.0 62.3 %tournament.1 = f32[4,128]{1,0:T(4,128)} custom-call(s32[4,32]{1,0:T(4,128)} %plan_in.1, bf16[512,1024]{1,0:T(8,128)(2,1)} %emb_in.1, s32[4,128]{1,0:T(4,128)} %bitcast.3), custom_call_target="tpu_custom_call" | custom-call | flops 4294967296 | bytes 1048576 | tf_op jit(solution)/shard_map/tournament/pallas_call | solution.py:471
  62.3 1.3 %copy.5 = f32[512]{0:T(512)} copy(f32[512]{0:T(512)} %bitcast.2) | data formatting | bytes 4096

commit v2 on v1

--- a/solution.py
+++ b/solution.py
@@ -18,6 +18,7 @@
 WAVE_ROWS = ROWS // WAVES
 CHUNK = WAVE_ROWS // SPOTS
 D = 1024
+FAR_FIRST = (10, 6, 14, 9, 11, 2, 8, 5, 7, 13, 15, 1, 3, 4, 12, 0)
 PARTS = 4
 PIECE = ROWS // PARTS
 
@@ -64,7 +65,6 @@
     col_max,
     col_sum,
     col_own,
-    col_in,
     col_table,
     load_s,
     one_s,
@@ -81,8 +81,6 @@
     idb_r,
     row_s,
     row_r,
-    cola_s,
-    cola_r,
     colb_s,
     colb_r,
 ):
@@ -98,6 +96,10 @@
 
     def spot_to(k):
         return ((z + k // 4) % 4) * 4 + (y + k % 4) % 4
+
+    def beside(side, k):
+        device_lo, device_hi = (lo + (side + 1) // 2) % 2, (hi + side // 2) % 2
+        return (device_lo * 16 + spot_to(k), device_hi * 2 + core)
 
     intra = ((1 - lo) * 16 + here, rep)
     inter = ((1 - lo) * 16 + here, (1 - hi) * 2 + core)
@@ -364,14 +366,14 @@
     forward(1).wait_recv()
     for pair in range(2):
         tile(0, pair, 3, 0, half)
+    for i in range(2, PARTS):
+        to_across(i).wait_recv()
+        forward(i).start()
     arrived(1, 0)
     tile(1, 0, 0, 0, ROWS)
     tile(1, 0, 1, 0, ROWS)
     tile(1, 0, 2, 0, half)
     tile(1, 0, 3, 0, half)
-    for i in range(2, PARTS):
-        to_across(i).wait_recv()
-        forward(i).start()
     for w, pair in ((0, 0), (0, 1), (1, 0)):
         tile(w, pair, 2, half, half)
     for i in range(2, PARTS):
@@ -384,11 +386,20 @@
         tile(1, 1, slot, 0, ROWS)
     finish_columns(1, 1)
 
-    def col_copy(j):
-        return remote(col_own, col_in.at[j], cola_s.at[j], cola_r.at[j], (intra, inter)[j])
-
-    col_copy(0).start()
-    col_copy(1).start()
+    def col_spread(side, k):
+        return remote(
+            col_own,
+            col_table.at[side, here],
+            colb_s.at[side, k],
+            colb_r.at[side, k],
+            beside(side, k),
+        )
+
+    for k in FAR_FIRST:
+        for side in (2, 1, 0):
+            if side or k:
+                col_spread(side, k).start()
+    col_table[0, here] = col_own[...]
 
     def row_copy(j):
         return remote(
@@ -406,49 +417,12 @@
             row_in[j, 4:8, :] = row_in[j, 0:4, :]
             row_copy(j).start()
 
-    for j in range(2):
-        col_copy(j).wait_recv()
-    col_table[here, 0] = col_own[...]
-    for pair in range(2):
-        source = place(hosted_mask(pair, (1 - lo) * 16 + here), here)[1]
-        odd = jnp.bitwise_and(jnp.right_shift(source, 2), 1)
-        for w in range(WAVES):
-            rows = slice(pair * 4 + w * 2, pair * 4 + w * 2 + 2)
-            col_table[here, 1, rows, :] = jnp.where(
-                odd == w, col_in[0, rows, :], col_in[1, rows, :]
-            )
-
-    def col_spread(k):
-        return remote(
-            col_table.at[here], col_table.at[here], colb_s.at[k], colb_r.at[k], at_spot(k)
-        )
-
-    loop(1, SPOTS, lambda k: col_spread(k).start())
-    loop(1, SPOTS, lambda k: col_spread(k).wait_recv())
-    for j in range(1, 4):
-        row_copy(j).wait_recv()
-
-    terms = [row_in[0, 0:4, :]]
-    for j in range(1, 4):
-        terms.append(row_in[3 + j, 0:4, :])
-    for pair in range(2):
-        side, source = place(guest_mask(pair, blk), here)
-        terms.append(col_table[source, side][pair * 4 : pair * 4 + 4, :])
-    top = terms[0]
-    for term in terms[1:]:
-        top = jnp.maximum(top, term)
-    total = jnp.exp2(terms[0] - top)
-    for term in terms[1:]:
-        total = total + jnp.exp2(term - top)
-    out[...] = (top + jnp.log2(total)) * UNSCALE
-
     def sent(k):
         id_spread(k).wait_send()
         for w in range(WAVES):
             spread(w, k).wait_send()
             for pair in range(2):
                 deliver(w, pair, k).wait_send()
-        col_spread(k).wait_send()
 
     loop(1, SPOTS, sent)
     for w in range(WAVES):
@@ -460,10 +434,37 @@
         forward(i).wait_send()
     for j in range(1, 6):
         id_copy(j).wait_send()
+
+    for side in range(3):
+        loop(0 if side else 1, SPOTS, lambda k, side=side: col_spread(side, k).wait_recv())
+    for j in range(1, 4):
+        row_copy(j).wait_recv()
+
+    for w in range(WAVES):
+        rows = slice(2 * w, 2 * w + 2)
+        terms = [row_in[0, rows, :]]
+        for j in range(1, 4):
+            terms.append(row_in[3 + j, rows, :])
+        for pair in range(2):
+            side, source = place(guest_mask(pair, blk), here)
+            rows = slice(pair * 4 + 2 * w, pair * 4 + 2 * w + 2)
+            near = col_table[0, source][rows, :]
+            even, odd = col_table[1, source][rows, :], col_table[2, source][rows, :]
+            terms.append(
+                jnp.where(side == 1, jnp.where((z + w) % 2 == 0, even, odd), near)
+            )
+        top = terms[0]
+        for term in terms[1:]:
+            top = jnp.maximum(top, term)
+        total = jnp.exp2(terms[0] - top)
+        for term in terms[1:]:
+            total = total + jnp.exp2(term - top)
+        out[2 * w : 2 * w + 2, :] = (top + jnp.log2(total)) * UNSCALE
+
+    for side in range(3):
+        loop(0 if side else 1, SPOTS, lambda k, side=side: col_spread(side, k).wait_send())
     for j in range(1, 4):
         row_copy(j).wait_send()
-    for j in range(2):
-        col_copy(j).wait_send()
 
 
 def shards(embeddings, doc_ids, plan):
@@ -491,8 +492,7 @@
             pltpu.VMEM((4, 8, WAVE_ROWS), jnp.float32),
             pltpu.VMEM((4, 8, WAVE_ROWS), jnp.float32),
             pltpu.VMEM((8, 128), jnp.float32),
-            pltpu.VMEM((2, 8, 128), jnp.float32),
-            pltpu.VMEM((SPOTS, 2, 8, 128), jnp.float32),
+            pltpu.VMEM((3, SPOTS, 8, 128), jnp.float32),
             sems((4,)),
             sems((WAVES, SPOTS)),
             sems((WAVES, SPOTS)),
@@ -508,10 +508,8 @@
             sems((SPOTS,)),
             sems((4,)),
             sems((4,)),
-            sems((2,)),
-            sems((2,)),
-            sems((SPOTS,)),
-            sems((SPOTS,)),
+            sems((3, SPOTS)),
+            sems((3, SPOTS)),
         ],
         compiler_params=pltpu.CompilerParams(
             collective_id=0, has_side_effects=True, vmem_limit_bytes=56 * 2**20

time: 64.1 us -> 62.3 us (0.972)
  Pallas kernels: 62.3 us -> 60.9 us
    pallas_call x1, Pallas kernels: 62.3 us -> 60.9 us  [shards(): pl.pallas_call(kernel, out_shape=jax.ShapeDtypeStruct((4, 128), jnp.float...]
where the time goes in v2:
time: 62.3 us; the launch traced here: 62.2 us
  Pallas kernels  60.9 us (98%)
  local copies, waits for them, and re-layouts  1.26 us (2%)
    pallas_call x1, Pallas kernels, shards(): pl.pallas_call(kernel, out_shape=jax.ShapeDtypeStruct((4, 128), jnp.float...  60.9 us
    unnamed x1, local copies, waits for them, and re-layouts  1.26 us

profile of v2, /device:TPU:0, one launch (start us, length us, event | category | flops | bytes accessed | tf_op | source)
XLA Modules:
  0.0 62.2 jit_solution(6074995343465852477)
XLA Ops:
  0.0 60.9 %tournament.1 = f32[4,128]{1,0:T(4,128)} custom-call(s32[4,32]{1,0:T(4,128)} %plan_in.1, bf16[512,1024]{1,0:T(8,128)(2,1)} %emb_in.1, s32[4,128]{1,0:T(4,128)} %bitcast.3), custom_call_target="tpu_custom_call" | custom-call | flops 4294967296 | bytes 1048576 | tf_op jit(solution)/shard_map/tournament/pallas_call | solution.py:472
  60.9 1.3 %copy.5 = f32[512]{0:T(512)} copy(f32[512]{0:T(512)} %bitcast.2) | data formatting | bytes 4096

commit v3 on v2

--- a/solution.py
+++ b/solution.py
@@ -18,6 +18,7 @@
 WAVE_ROWS = ROWS // WAVES
 CHUNK = WAVE_ROWS // SPOTS
 D = 1024
+NEAR_FIRST = (3, 4, 12, 1, 8, 7, 15, 5, 13, 2, 11, 6, 9, 14, 10)
 FAR_FIRST = (10, 6, 14, 9, 11, 2, 8, 5, 7, 13, 15, 1, 3, 4, 12, 0)
 PARTS = 4
 PIECE = ROWS // PARTS
@@ -259,18 +260,19 @@
             outbox[w, pair, k] = held[w][side, source]
             deliver(w, pair, k).start()
 
-        loop(1, SPOTS, send_rows)
+        for k in NEAR_FIRST:
+            send_rows(k)
         side, source = place(hosted_mask(pair, blk), here)
         right[w, pair, here] = held[w][side, source]
 
     for w in range(WAVES):
         for dz in range(4):
             hand(w, dz).wait_recv()
-        if w == WAVES - 1:
-            for i in range(1, PARTS):
-                to_across(i).start()
         for pair in range(2):
+            if w == WAVES - 1:
+                to_across(1 + pair).start()
             deliver_all(w, pair)
+    to_across(3).start()
 
     for j in range(4):
         for g in range(4):

time: 62.3 us -> 62.3 us (level)
  no operation moved by 1% of the time
where the time goes in v3:
time: 62.3 us; the launch traced here: 62.2 us
  Pallas kernels  60.9 us (98%)
  local copies, waits for them, and re-layouts  1.26 us (2%)
    pallas_call x1, Pallas kernels, shards(): pl.pallas_call(kernel, out_shape=jax.ShapeDtypeStruct((4, 128), jnp.float...  60.9 us
    unnamed x1, local copies, waits for them, and re-layouts  1.26 us

profile of v3, /device:TPU:0, one launch (start us, length us, event | category | flops | bytes accessed | tf_op | source)
XLA Modules:
  0.0 62.2 jit_solution(15093269097781260605)
XLA Ops:
  0.0 60.9 %tournament.1 = f32[4,128]{1,0:T(4,128)} custom-call(s32[4,32]{1,0:T(4,128)} %plan_in.1, bf16[512,1024]{1,0:T(8,128)(2,1)} %emb_in.1, s32[4,128]{1,0:T(4,128)} %bitcast.3), custom_call_target="tpu_custom_call" | custom-call | flops 4294967296 | bytes 1048576 | tf_op jit(solution)/shard_map/tournament/pallas_call | solution.py:474
  60.9 1.3 %copy.5 = f32[512]{0:T(512)} copy(f32[512]{0:T(512)} %bitcast.2) | data formatting | bytes 4096

commit v4 on v2

--- a/solution.py
+++ b/solution.py
@@ -248,7 +248,7 @@
             outbox.at[w, pair, k],
             right.at[w, pair, here],
             two_s.at[w, pair, k],
-            two_r.at[w, pair, k],
+            two_r.at[w, pair],
             at_spot(k),
         )
 
@@ -348,7 +348,8 @@
             col_own[row : row + 1, :] = result[:, g * 128 : (g + 1) * 128]
 
     def arrived(w, pair):
-        loop(1, SPOTS, lambda k: deliver(w, pair, k).wait_recv())
+        some = right.at[w, pair, pl.ds(0, SPOTS - 1)]
+        remote(some, some, two_s.at[w, pair, 0], two_r.at[w, pair], at_spot(1)).wait_recv()
 
     to_across(0).wait_recv()
     forward(0).start()
@@ -391,7 +392,7 @@
             col_own,
             col_table.at[side, here],
             colb_s.at[side, k],
-            colb_r.at[side, k],
+            colb_r.at[side],
             beside(side, k),
         )
 
@@ -436,7 +437,8 @@
         id_copy(j).wait_send()
 
     for side in range(3):
-        loop(0 if side else 1, SPOTS, lambda k, side=side: col_spread(side, k).wait_recv())
+        some = col_table.at[side, pl.ds(0, SPOTS if side else SPOTS - 1)]
+        remote(some, some, colb_s.at[side, 0], colb_r.at[side], at_spot(1)).wait_recv()
     for j in range(1, 4):
         row_copy(j).wait_recv()
 
@@ -499,7 +501,7 @@
             sems((WAVES, 4)),
             sems((WAVES, 4)),
             sems((WAVES, 2, SPOTS)),
-            sems((WAVES, 2, SPOTS)),
+            sems((WAVES, 2)),
             sems((1 + 2 * PARTS,)),
             sems((1 + 2 * PARTS,)),
             sems((6,)),
@@ -509,7 +511,7 @@
             sems((4,)),
             sems((4,)),
             sems((3, SPOTS)),
-            sems((3, SPOTS)),
+            sems((3,)),
         ],
         compiler_params=pltpu.CompilerParams(
             collective_id=0, has_side_effects=True, vmem_limit_bytes=56 * 2**20

time: 62.3 us -> 61.6 us (0.989)
  Pallas kernels: 60.9 us -> 60.2 us
    pallas_call x1, Pallas kernels: 60.9 us -> 60.2 us  [shards(): pl.pallas_call(kernel, out_shape=jax.ShapeDtypeStruct((4, 128), jnp.float...]
where the time goes in v4:
time: 61.6 us; the launch traced here: 61.5 us
  Pallas kernels  60.2 us (98%)
  local copies, waits for them, and re-layouts  1.26 us (2%)
    pallas_call x1, Pallas kernels, shards(): pl.pallas_call(kernel, out_shape=jax.ShapeDtypeStruct((4, 128), jnp.float...  60.2 us
    unnamed x1, local copies, waits for them, and re-layouts  1.26 us

profile of v4, /device:TPU:0, one launch (start us, length us, event | category | flops | bytes accessed | tf_op | source)
XLA Modules:
  0.0 61.5 jit_solution(6406660225912474592)
XLA Ops:
  0.0 60.2 %tournament.1 = f32[4,128]{1,0:T(4,128)} custom-call(s32[4,32]{1,0:T(4,128)} %plan_in.1, bf16[512,1024]{1,0:T(8,128)(2,1)} %emb_in.1, s32[4,128]{1,0:T(4,128)} %bitcast.3), custom_call_target="tpu_custom_call" | custom-call | flops 4294967296 | bytes 1048576 | tf_op jit(solution)/shard_map/tournament/pallas_call | solution.py:474
  60.2 1.3 %copy.5 = f32[512]{0:T(512)} copy(f32[512]{0:T(512)} %bitcast.2) | data formatting | bytes 4096
